TPU v7x, 256 devices: a whole 4x4x8 slice. The times are simulated.
256 devices in a mesh: fsdp: 64 (over z, x, y_hi), tp: 4 (over y_lo, core).
Axes of the slice: x: 4, y: 4 (y_hi: 2, y_lo: 2; y = y_hi * 2 + y_lo), z: 8, core: 2. Of those that a mesh axis runs over, the one named last changes fastest.
Arguments:
- tokens: bfloat16 [256, 8192], P('fsdp', 'tp'), may hold values from -6 to 6
- token_adapter_index: int32 [256], replicated, may hold values from 0 to 3
- gate_projection_weight: bfloat16 [8192, 16384], P('tp', 'fsdp'), may hold values from -0.0625 to 0.0625
- up_projection_weight: bfloat16 [8192, 16384], P('tp', 'fsdp'), may hold values from -0.0625 to 0.0625
- down_projection_weight: bfloat16 [16384, 8192], P('fsdp', 'tp'), may hold values from -0.046875 to 0.046875
- adapter_input_maps: bfloat16 [4, 64, 8192], P(None, None, 'tp'), may hold values from -0.0625 to 0.0625
- adapter_output_maps: bfloat16 [4, 64, 16384], P(None, None, 'fsdp'), may hold values from -0.75 to 0.75
- cotangent: bfloat16 [256, 8192], P('fsdp', 'tp'), may hold values from -6 to 6
Outputs:
- reference_out: bfloat16 [256, 8192], P('fsdp', 'tp')
- policy_out: bfloat16 [256, 8192], P('fsdp', 'tp')
- input_map_gradient: float32 [4, 64, 8192], P(None, None, 'tp')
- output_map_gradient: float32 [4, 64, 16384], P(None, None, 'fsdp')
All inputs are finite; a program needn't handle non-finite values.
Results may differ from a plain program's by a relative error of at most 0.015.
Values may be sent and summed in bfloat16 or wider, within the bound.
A program may use at most 64 MiB of HBM per device.

v0:
```python
import jax
import jax.numpy as jnp
from jax import lax
from jax.sharding import PartitionSpec as P


def widen_rank(values, adapter_indicator):
    count = values.shape[0]
    return (
        (adapter_indicator[:, :, None] * values[:, None, :].astype(jnp.float32))
        .reshape(count, -1)
        .astype(jnp.bfloat16)
    )


def adapter_selection(wide, adapter_indicator):
    count = wide.shape[0]
    return jnp.einsum(
        "mj,mjr->mr", adapter_indicator, wide.reshape(count, adapter_indicator.shape[1], -1)
    )


def contract_trailing(left, right):
    return lax.dot_general(
        left, right, (((1,), (1,)), ((), ())), preferred_element_type=jnp.float32
    )


def contract_leading(left, right):
    return lax.dot_general(
        left, right, (((0,), (0,)), ((), ())), preferred_element_type=jnp.float32
    )


def body(
    tokens,
    token_adapter_index,
    gate_projection_weight,
    up_projection_weight,
    down_projection_weight,
    adapter_input_maps,
    adapter_output_maps,
    cotangent,
):
    adapter_list, adapter_rank_rows, width_slice = adapter_input_maps.shape
    hidden_slice = adapter_output_maps.shape[2]
    adapter_indicator = (
        token_adapter_index[:, None] == jnp.arange(adapter_list, dtype=jnp.int32)[None, :]
    ).astype(jnp.float32)
    collected_rows = lax.all_gather(tokens, "fsdp", axis=0, tiled=True)
    gate_piece = jnp.dot(collected_rows, gate_projection_weight, preferred_element_type=jnp.float32)
    up_piece = jnp.dot(collected_rows, up_projection_weight, preferred_element_type=jnp.float32)
    stacked_input_maps = adapter_input_maps.reshape(adapter_list * adapter_rank_rows, width_slice)
    stacked_output_maps = adapter_output_maps.reshape(
        adapter_list * adapter_rank_rows, hidden_slice
    )
    adapter_piece = adapter_selection(
        contract_trailing(collected_rows, stacked_input_maps), adapter_indicator
    )
    gate_values, up_complete, adapter_total_sum = lax.psum(
        (gate_piece, up_piece, adapter_piece), "tp"
    )
    adapter_widened = widen_rank(adapter_total_sum.astype(jnp.bfloat16), adapter_indicator)
    activated = jax.nn.silu(gate_values)
    up_policy_values = up_complete + jnp.dot(
        adapter_widened, stacked_output_maps, preferred_element_type=jnp.float32
    )
    hidden_ref = (activated * up_complete).astype(jnp.bfloat16)
    hidden_pol = (activated * up_policy_values).astype(jnp.bfloat16)
    summed = lax.psum_scatter(
        jnp.concatenate(
            [
                jnp.dot(hidden_ref, down_projection_weight, preferred_element_type=jnp.float32),
                jnp.dot(hidden_pol, down_projection_weight, preferred_element_type=jnp.float32),
            ],
            axis=1,
        ),
        "fsdp",
        scatter_dimension=0,
        tiled=True,
    )
    reference_out = summed[:, :width_slice].astype(jnp.bfloat16)
    policy_out = summed[:, width_slice:].astype(jnp.bfloat16)
    grad_part = contract_trailing(
        lax.all_gather(cotangent, "fsdp", axis=0, tiled=True), down_projection_weight
    )
    grad_hidden = lax.psum(grad_part, "tp")
    up_gradient = (grad_hidden * activated).astype(jnp.bfloat16)
    output_map_gradient = contract_leading(adapter_widened, up_gradient).reshape(
        adapter_list, adapter_rank_rows, hidden_slice
    )
    backward_piece = adapter_selection(
        contract_trailing(up_gradient, stacked_output_maps), adapter_indicator
    )
    backward_share = lax.psum_scatter(backward_piece, "fsdp", scatter_dimension=0, tiled=True)
    adapter_backward = lax.all_gather(
        backward_share.astype(jnp.bfloat16), "fsdp", axis=0, tiled=True
    )
    backward_widened = widen_rank(adapter_backward, adapter_indicator)
    input_map_gradient = contract_leading(backward_widened, collected_rows).reshape(
        adapter_list, adapter_rank_rows, width_slice
    )
    return (reference_out, policy_out, input_map_gradient, output_map_gradient)


def solution(mesh):
    in_specs = (
        P("fsdp", "tp"),
        P(),
        P("tp", "fsdp"),
        P("tp", "fsdp"),
        P("fsdp", "tp"),
        P(None, None, "tp"),
        P(None, None, "fsdp"),
        P("fsdp", "tp"),
    )
    out_specs = (P("fsdp", "tp"), P("fsdp", "tp"), P(None, None, "tp"), P(None, None, "fsdp"))
    return jax.shard_map(body, mesh=mesh, in_specs=in_specs, out_specs=out_specs, check_vma=False)
```

profile of v0, /device:TPU:32, one launch (start us, length us, event | category | flops | bytes accessed | tf_op | source)
XLA Modules:
  0.0 881.5 jit_solution(13359263538953637937)
XLA Ops:
  7.2 0.7 all-gather.6.cloned.1.call-update
  8.0 0.7 all-gather.8.cloned.1.call-update
  8.7 118.3 %all-gather.6.cloned.1.call-done = bf16[64,4,2048]{2,1,0:T(4,128)(2,1)} async-done(((bf16[1,4,2048]{2,1,0:T(4,128)(2,1)}), bf16[64,4,2048]{2,1,0:T(4,128)(2,1)}) %all-gather.6.cloned.1.call-update) | async-done | bytes 1048592 | tf_op jit(solution)/shard_map/all_gather | solution.py:50
  127.0 1.3 reshape.58
  128.4 1.1 fusion.26
  129.6 1.1 fusion.25
  130.8 110.4 %all-gather.8.cloned.1.call-done = bf16[64,4,2048]{2,1,0:T(4,128)(2,1)} async-done(((bf16[1,4,2048]{2,1,0:T(4,128)(2,1)}), bf16[64,4,2048]{2,1,0:T(4,128)(2,1)}) %all-gather.8.cloned.1.call-update) | async-done | bytes 1048592 | tf_op jit(solution)/shard_map/all_gather | solution.py:85
  241.2 1.3 reshape.60
  242.6 1.2 fusion.27
  245.4 2.1 fusion.3
  247.5 11.7 %psum.30 = bf16[256,64]{0,1:T(8,128)(2,1)S(1)} all-reduce(f32[256,64]{0,1:T(8,128)S(1)} %fusion.3), channel_id=1, replica_groups=mesh['fsdp'=64,'tp'=4] {'tp'}, use_global_device_ids=true, to_apply=%region_2.0 | all-reduce | flops 16384 | bytes 98304 | tf_op jit(solution)/shard_map/psum | solution.py:60
  259.2 27.8 %all-reduce.7.cloned.1.call-done = (f32[256,256]{1,0:T(8,128)}, f32[256,256]{1,0:T(8,128)}, f32[256,256]{1,0:T(8,128)}) async-done(((f32[256,256]{1,0:T(8,128)}, f32[256,256]{1,0:T(8,128)}, f32[256,256]{1,0:T(8,128)}), (f32[256,256]{1,0:T(8,128)}, f32[256,256]{1,0:T(8,128)}, f32[256,256]{1,0:T(8,128)})) %all-reduce.7.cloned.1.call-update) | async-done | bytes 786448 | tf_op jit(solution)/shard_map/psum | solution.py:60
  287.1 1.1 fusion.10
  288.2 0.9 fusion.4
  289.0 0.9 fusion.7
  289.9 2.9 fusion.5
  292.9 1.4 fusion.9
  294.3 0.9 copy.22
  295.2 3.9 pad_maximum_fusion
  299.1 398.7 %all-reduce.8 = (bf16[256,4096]{1,0:T(8,128)(2,1)}, bf16[256,64]{1,0:T(8,128)(2,1)S(1)}) all-reduce(f32[256,4096]{1,0:T(8,128)} %pad_maximum_fusion, f32[256,64]{1,0:T(8,128)S(1)} %copy.22), channel_id=2, replica_groups=mesh['fsdp'=64,'tp'=4] {'fsdp'}, use_global_device_ids=true, to_apply=%region_3.4.clone | all-reduce | flops 1064960 | bytes 6389760
  697.8 0.9 dynamic-slice_convert_fusion
  698.7 0.6 fusion.24
  699.3 173.8 %all-gather.2 = bf16[64,4,64]{2,1,0:T(4,128)(2,1)S(1)} all-gather(bf16[1,4,64]{2,1,0:T(4,128)(2,1)S(1)} %fusion.23), channel_id=1, replica_groups=mesh['fsdp'=64,'tp'=4] {'fsdp'}, dimensions={0}, use_global_device_ids=true | all-gather | bytes 33280 | tf_op jit(solution)/shard_map/all_gather | solution.py:96
  873.2 1.8 fusion.12
  (30 shorter events, 1.2 us)
Async XLA Ops:
  7.2 235.4 %copy-start = (bf16[256,2048]{1,0:T(8,128)(2,1)S(1)}, bf16[256,2048]{1,0:T(8,128)(2,1)}, u32[]{:S(2)}) copy-start(bf16[256,2048]{1,0:T(8,128)(2,1)} %param.12) | copy-start | bytes 3145732
  7.2 121.2 %copy-start.5 = (bf16[2048,256]{1,0:T(8,128)(2,1)S(1)}, bf16[2048,256]{1,0:T(8,128)(2,1)}, u32[]{:S(2)}) copy-start(bf16[2048,256]{1,0:T(8,128)(2,1)} %param.11) | copy-start | bytes 3145732
  7.2 119.8 %all-gather.6.cloned.1.call-start = ((), (), s32[]{:S(2)}) async-start(), calls=%async_computation | async-start | bytes 1064960 | tf_op jit(solution)/shard_map/all_gather | solution.py:50
  7.9 233.3 %all-gather.8.cloned.1.call-start = ((), (), s32[]{:S(2)}) async-start(), calls=%async_computation.1 | async-start | bytes 1064960 | tf_op jit(solution)/shard_map/all_gather | solution.py:85
  8.7 278.4 %all-reduce.7.cloned.1.call-start = ((), (), s32[]{:S(2)}) async-start(), calls=%async_computation.2 | async-start | bytes 1572864 | tf_op jit(solution)/shard_map/psum | solution.py:60
  128.4 1.2 copy-start.6
  242.6 1.3 copy-start.9
  242.6 2.5 copy-start.8
  242.6 2.5 copy-start.1
  245.4 43.7 %copy-start.2 = (bf16[256,2048,1]{1,0,2:T(8,128)(2,1)}, bf16[256,2048,1]{1,0,2:T(8,128)(2,1)S(1)}, u32[]{:S(2)}) copy-start(bf16[256,2048,1]{1,0,2:T(8,128)(2,1)S(1)} %reshape.64) | copy-start | bytes 3145732
  245.4 42.8 %copy-start.7 = (bf16[4,64,256]{2,1,0:T(8,128)(2,1)S(1)}, bf16[4,64,256]{2,1,0:T(8,128)(2,1)}, u32[]{:S(2)}) copy-start(bf16[4,64,256]{2,1,0:T(8,128)(2,1)} %param.14) | copy-start | bytes 393220
  289.0 3.8 copy-start.4
  299.1 574.1 %copy-start.3 = (bf16[256,2048,1]{1,0,2:T(8,128)(2,1)S(1)}, bf16[256,2048,1]{1,0,2:T(8,128)(2,1)}, u32[]{:S(2)}) copy-start(bf16[256,2048,1]{1,0,2:T(8,128)(2,1)} %copy-done.2) | copy-start | bytes 3145732
Sparse Core Ops, SparseCore 0:
  11.6 115.3 all-gather.5
  130.6 110.5 all-gather.7
  244.7 42.3 all-reduce.6
where the time goes:
time: 897 us; the launch traced here: 882 us
  blocking collectives  584 us (65%)
  waiting for transfers between devices  258 us (29%)
  between operations  14.6 us (2%)
  matrix products  13.4 us (1%)
    unnamed x1, blocking collectives  399 us
    all_gather x1, blocking collectives, body(): lax.all_gather(backward_share.astype(jnp.bfloat16), 'fsdp', axis=0, tiled...  174 us
    all_gather x1, waiting for transfers between devices, body(): collected_rows = lax.all_gather(tokens, 'fsdp', axis=0, tiled=True)  118 us
    all_gather x1, waiting for transfers between devices, body(): lax.all_gather(cotangent, 'fsdp', axis=0, tiled=True)  110 us
    psum x1, waiting for transfers between devices, body(): lax.psum((gate_piece, up_piece, adapter_piece), 'tp')  27.8 us
  transfers between devices with their start and end apart: 3, of which 3 were waited for; matrix products, arithmetic and copies ran while one was open for 1% of the time, Pallas kernels for 0%

commit v1 on v0

v1 whole, which is shorter than its diff:
```python
import functools

import jax
import jax.numpy as jnp
from jax import lax
from jax.experimental import pallas as pl
from jax.experimental.pallas import tpu as pltpu
from jax.sharding import PartitionSpec as P

MESH = pl.DeviceIdType.MESH
BF = jnp.bfloat16
F32 = jnp.float32

GROUPS = (("z", 0, 512), ("p", 512, 768), ("p", 1280, 768))


def nt(a, b):
    return lax.dot_general(a, b, (((1,), (1,)), ((), ())), preferred_element_type=F32)


def tn(a, b):
    return lax.dot_general(a, b, (((0,), (0,)), ((), ())), preferred_element_type=F32)


def nn(a, b):
    return jnp.dot(a, b, preferred_element_type=F32)


def iota2(n, m):
    return (
        lax.broadcasted_iota(jnp.int32, (n, m), 0),
        lax.broadcasted_iota(jnp.int32, (n, m), 1),
    )


def as_matrix(condition):
    return condition.astype(F32).astype(BF)


def kernel(
    idx, tok, cot, gate, up, down, imaps, omaps,
    ref_out, pol_out, in_grad, out_grad,
    gate_v, up_v, down_v, imaps_v, omaps_v,
    ta, tb, ca, cb, xt, ct,
    f1, s1, r1, s2, r2, e1, er1,
    f2, g1, gr1, g2, gr2, e2, er2,
    act_v, mask_v, lw_v, href, hpol, gup, hrp, hpp,
    ar0, ar1, ar1s, ar2, ar2s, ar3,
    in_v, out_v,
    *rest,
):
    ngroups = len(GROUPS)
    ysend, yrecv, zsend, zrecv = (rest[i * ngroups : (i + 1) * ngroups] for i in range(4))
    wsem, ssem, rsem, osem = rest[4 * ngroups :]

    f = lax.axis_index("fsdp")
    t = lax.axis_index("tp")
    z, p, x, h, c = f // 8, f % 8, (f // 2) % 4, f % 2, t % 2

    def zdev(k):
        return {"fsdp": lax.rem(z + k + 8, 8) * 8 + p, "tp": t}

    def pidx(k):
        return lax.rem(x + k // 2, 4) * 2 + (h + k % 2) % 2

    def pdev(k):
        return {"fsdp": z * 8 + pidx(k), "tp": t}

    def tdev(k):
        return {"fsdp": f, "tp": ((t // 2 + k // 2) % 2) * 2 + (c + k % 2) % 2}

    counter = [0]
    pending = []

    def send(src, dst, device):
        n = counter[0]
        counter[0] += 1
        copy = pltpu.make_async_remote_copy(
            src_ref=src, dst_ref=dst, send_sem=ssem.at[n], recv_sem=rsem.at[n],
            device_id=device, device_id_type=MESH,
        )
        copy.start()
        pending.append(copy)
        return copy

    loads = []
    for n, (src, dst) in enumerate(
        ((gate, gate_v), (up, up_v), (imaps, imaps_v), (omaps, omaps_v), (down, down_v))
    ):
        load = pltpu.make_async_copy(src, dst, wsem.at[n])
        load.start()
        loads.append(load)

    barrier = pltpu.get_barrier_semaphore()
    partners = [zdev(k) for k in range(1, 8)] + [pdev(k) for k in range(1, 8)] + [tdev(k) for k in range(1, 4)]
    for device in partners:
        pl.semaphore_signal(barrier, 1, device_id=device, device_id_type=MESH)

    i16, j4 = iota2(16, 4)
    for src, half_a, half_b in ((tok, ta, tb), (cot, ca, cb)):
        packed = None
        for q in range(4):
            spread = as_matrix(i16 == q * 4 + j4)
            term = nn(spread, src[:, q * 512 : (q + 1) * 512])
            packed = term if packed is None else packed + term
        packed = packed.astype(BF)
        half_a[z, p] = packed[:, :256]
        half_b[z, p] = packed[:, 256:]

    i8, j8 = iota2(8, 256)
    chosen = as_matrix(idx[...] == i8)
    mask_v[...] = tn(chosen, as_matrix(i8 == j8 // 64)).astype(BF)

    pl.semaphore_wait(barrier, len(partners))

    def first_hops(half_a, half_b):
        a = [send(half_a.at[z, p], half_a.at[z, p], pdev(k)) for k in range(1, 8)]
        b = [send(half_b.at[z, p], half_b.at[z, p], zdev(k)) for k in range(1, 8)]
        return a, b

    def second_hops(half_a, half_b, first):
        a, b = first
        for copy in a:
            copy.wait_recv()
        near = [send(half_a.at[z], half_a.at[z], zdev(k)) for k in (2, -2, 1, -1)]
        for copy in b:
            copy.wait_recv()
        plane = [send(half_b.at[:, p], half_b.at[:, p], pdev(k)) for k in range(1, 8)]
        return near, plane

    def third_hops(half_a, second):
        near, _ = second
        far = []
        for n, sign in ((0, 1), (1, -1)):
            near[n].wait_recv()
            block = lax.rem(z - 2 * sign + 8, 8)
            part = half_a.at[block, pl.ds(0 if sign == 1 else 4, 4)]
            far.append(send(part, part, zdev(2 * sign)))
            far.append(send(half_a.at[block], half_a.at[block], zdev(sign)))
        return far

    def finish(second, far):
        near, plane = second
        for copy in near[2:] + plane + far:
            copy.wait_recv()

    first_t = first_hops(ta, tb)
    first_c = first_hops(ca, cb)
    second_t = second_hops(ta, tb, first_t)
    far_t = third_hops(ta, second_t)
    second_c = second_hops(ca, cb, first_c)

    i256, j256 = iota2(256, 256)
    spread16 = as_matrix(j256 == ((i256 // 4) % 16) * 16 + (i256 // 64) * 4 + i256 % 4)
    plane_major = as_matrix(j256 == ((i256 // 4) % 8) * 32 + (i256 // 32) * 4 + i256 % 4)
    ifold, jfold = iota2(256, 128)
    fold_lo = as_matrix(ifold % 64 == jfold)
    fold_hi = as_matrix(ifold % 64 + 64 == jfold)
    i128, j128 = iota2(128, 128)
    regroup = as_matrix(
        j128 == ((i128 // 4) % 2) * 64 + ((i128 // 8) % 2) * 32 + (i128 // 16) * 4 + i128 % 4
    )

    def unpack(half_a, half_b, whole):
        for g in range(4):
            for n, half in enumerate((half_a, half_b)):
                block = half[2 * g : 2 * g + 2].reshape(256, 256)
                rows = nn(spread16, block).astype(BF)
                for q in range(4):
                    whole[g * 64 : (g + 1) * 64, q * 512 + n * 256 : q * 512 + (n + 1) * 256] = rows[
                        q * 64 : (q + 1) * 64
                    ]

    finish(second_t, far_t)
    unpack(ta, tb, xt)
    for load in loads[:3]:
        load.wait()
    f1[:, 0:256] = nn(xt[...], gate_v[...])
    f1[:, 256:512] = nn(xt[...], up_v[...])
    low = (nt(xt[...], imaps_v[...]) * mask_v[...].astype(F32)).astype(BF)
    f1[:, 512:640] = nn(low, fold_lo)

    own = pl.ds(pl.multiple_of(c * 128, 128), 128)
    other = pl.ds(pl.multiple_of((1 - c) * 128, 128), 128)

    s1[...] = f1[other, :].astype(BF)
    core_t = send(s1, r1, tdev(1))
    far_c = third_hops(ca, second_c)
    core_t.wait_recv()
    s2[...] = (f1[own, :] + r1[...].astype(F32)).astype(BF)
    line_t = send(s2, r2, tdev(2))

    finish(second_c, far_c)
    unpack(ca, cb, ct)
    for load in loads[3:]:
        load.wait()
    f2[...] = nt(ct[...], down_v[...])
    g1[...] = f2[other, :].astype(BF)
    core_c = send(g1, gr1, tdev(1))

    line_t.wait_recv()
    total = s2[...].astype(F32) + r2[...].astype(F32)
    gate_values = total[:, 0:256]
    up_values = total[:, 256:512]
    lora_in = total[:, 512:640].astype(BF)
    wide = (nt(lora_in, fold_lo) * mask_v[own, :].astype(F32)).astype(BF)
    activated = gate_values / (1.0 + jnp.exp(-gate_values))
    act_v[...] = activated
    up_policy = up_values + nn(wide, omaps_v[...])
    e1[:, 0:256] = (activated * up_values).astype(BF)
    e1[:, 256:512] = (activated * up_policy).astype(BF)
    e1[:, 512:640] = lora_in
    pair_t = send(e1, er1, tdev(1))

    core_c.wait_recv()
    g2[...] = (f2[own, :] + gr1[...].astype(F32)).astype(BF)
    line_c = send(g2, gr2, tdev(2))

    href[own, :] = e1[:, 0:256]
    hpol[own, :] = e1[:, 256:512]
    lw_v[own, :] = wide
    pair_t.wait_recv()
    href[other, :] = er1[:, 0:256]
    hpol[other, :] = er1[:, 256:512]
    lw_v[other, :] = (nt(er1[:, 512:640], fold_lo) * mask_v[other, :].astype(F32)).astype(BF)
    hrp[...] = nn(plane_major, href[...]).astype(BF)
    hpp[...] = nn(plane_major, hpol[...]).astype(BF)

    stage1 = []
    for n, (kind, start, width) in enumerate(GROUPS):
        pair = (href, hpol) if kind == "z" else (hrp, hpp)
        for o in range(2):
            for q in range(2):
                half = width // 2
                block = nn(pair[o][...], down_v[:, start + q * half : start + (q + 1) * half]).astype(BF)
                ysend[n][:, o, :, q * half : (q + 1) * half] = block.reshape(8, 32, half)
        me = z if kind == "z" else p
        copies = []
        for k in range(1, 8):
            to = lax.rem(z + k, 8) if kind == "z" else pidx(k)
            copies.append(
                send(ysend[n].at[to], yrecv[n].at[me], zdev(k) if kind == "z" else pdev(k))
            )
        yrecv[n][me] = ysend[n][me]
        stage1.append(copies)

    line_c.wait_recv()
    grad = g2[...].astype(F32) + gr2[...].astype(F32)
    e2[...] = (grad * act_v[...]).astype(BF)
    pair_c = send(e2, er2, tdev(1))
    gup[own, :] = e2[...]
    pair_c.wait_recv()
    gup[other, :] = er2[...]

    mine = pl.ds(pl.multiple_of(t * 64, 64), 64)
    back = (nt(gup[mine, :], omaps_v[...]) * mask_v[mine, :].astype(F32)).astype(BF)
    ar0[...] = (nn(back[:32], fold_lo) + nn(back[32:], fold_hi)).astype(BF)
    ar1[p] = ar0[...]
    sum1 = [send(ar0, ar1.at[p], pdev(k)) for k in range(1, 8)]
    out_v[...] = tn(lw_v[...], gup[...])
    out_copy = pltpu.make_async_copy(out_v, out_grad, osem.at[0])
    out_copy.start()
    for copy in sum1:
        copy.wait_recv()
    ar1s[...] = jnp.sum(ar1[...].astype(F32), axis=0).astype(BF)
    ar2[z] = ar1s[...]
    sum2 = [send(ar1s, ar2.at[z], zdev(k)) for k in range(1, 8)]
    for copy in sum2:
        copy.wait_recv()
    ar2s[...] = jnp.sum(ar2[...].astype(F32), axis=0).astype(BF)
    ar3[t] = ar2s[...]
    sum3 = [send(ar2s, ar3.at[t], tdev(k)) for k in range(1, 4)]

    stage2 = []
    for n, (kind, start, width) in enumerate(GROUPS):
        half = width // 2
        for copy in stage1[n]:
            copy.wait_recv()
        pieces = []
        for q in range(2):
            for o in range(2):
                piece = yrecv[n][:, o, :, q * half : (q + 1) * half].astype(F32)
                pieces.append(jnp.sum(piece, axis=0).astype(BF))
        stacked = jnp.concatenate(pieces, axis=0)
        zsend[n][...] = nn(regroup, stacked).astype(BF).reshape(8, 16, half)
        me = p if kind == "z" else z
        copies = []
        for k in range(1, 8):
            to = pidx(k) if kind == "z" else lax.rem(z + k, 8)
            copies.append(
                send(zsend[n].at[to], zrecv[n].at[me], pdev(k) if kind == "z" else zdev(k))
            )
        zrecv[n][me] = zsend[n][me]
        stage2.append(copies)

    for copy in sum3:
        copy.wait_recv()
    wides = []
    for k in range(4):
        for fold in (fold_lo, fold_hi):
            wides.append(nt(ar3[k], fold))
    back_wide = (jnp.concatenate(wides, axis=0) * mask_v[...].astype(F32)).astype(BF)
    in_copies = []
    for k in range(4):
        in_v[:, k * 512 : (k + 1) * 512] = tn(back_wide, xt[:, k * 512 : (k + 1) * 512])
        copy = pltpu.make_async_copy(
            in_v.at[:, pl.ds(k * 512, 512)], in_grad.at[:, pl.ds(k * 512, 512)], osem.at[1 + k]
        )
        copy.start()
        in_copies.append(copy)

    i4, j16 = iota2(4, 16)
    for n, (kind, start, width) in enumerate(GROUPS):
        half = width // 2
        for copy in stage2[n]:
            copy.wait_recv()
        total = jnp.sum(zrecv[n][...].astype(F32), axis=0).astype(BF)
        for o, out in enumerate((ref_out, pol_out)):
            for q in range(2):
                pick = as_matrix(j16 == o * 8 + q * 4 + i4)
                out[:, start + q * half : start + (q + 1) * half] = nn(pick, total).astype(BF)

    out_copy.wait()
    for copy in in_copies:
        copy.wait()
    for copy in pending:
        copy.wait_send()


COPIES = 2 * (14 + 11 + 4) + 6 + 17 + 14 * len(GROUPS)


def body(tokens, token_adapter_index, gate, up, down, imaps, omaps, cotangent):
    adapters, rank, width = imaps.shape
    hidden = omaps.shape[2]
    vmem = pl.BlockSpec(memory_space=pltpu.VMEM)
    hbm = pl.BlockSpec(memory_space=pl.ANY)
    v = pltpu.VMEM
    scratch = [
        v((2048, 256), BF), v((2048, 256), BF), v((256, 2048), BF), v((256, 2048), BF), v((256, 256), BF),
        v((8, 8, 16, 256), BF), v((8, 8, 16, 256), BF), v((8, 8, 16, 256), BF), v((8, 8, 16, 256), BF),
        v((256, 2048), BF), v((256, 2048), BF),
        v((256, 640), F32), v((128, 640), BF), v((128, 640), BF), v((128, 640), BF), v((128, 640), BF),
        v((128, 640), BF), v((128, 640), BF),
        v((256, 256), F32), v((128, 256), BF), v((128, 256), BF), v((128, 256), BF), v((128, 256), BF),
        v((128, 256), BF), v((128, 256), BF),
        v((128, 256), F32), v((256, 256), BF), v((256, 256), BF), v((256, 256), BF), v((256, 256), BF),
        v((256, 256), BF), v((256, 256), BF), v((256, 256), BF),
        v((32, 128), BF), v((8, 32, 128), BF), v((32, 128), BF), v((8, 32, 128), BF), v((32, 128), BF),
        v((4, 32, 128), BF),
        v((256, 2048), F32), v((256, 256), F32),
    ]
    scratch += [v((8, 2, 32, w), BF) for _, _, w in GROUPS] * 2
    scratch += [v((8, 16, w // 2), BF) for _, _, w in GROUPS] * 2
    scratch += [
        pltpu.SemaphoreType.DMA((5,)),
        pltpu.SemaphoreType.DMA((COPIES,)),
        pltpu.SemaphoreType.DMA((COPIES,)),
        pltpu.SemaphoreType.DMA((5,)),
    ]
    ref_out, pol_out, in_grad, out_grad = pl.pallas_call(
        kernel,
        out_shape=(
            jax.ShapeDtypeStruct((4, width), BF),
            jax.ShapeDtypeStruct((4, width), BF),
            jax.ShapeDtypeStruct((adapters * rank, width), F32),
            jax.ShapeDtypeStruct((adapters * rank, hidden), F32),
        ),
        in_specs=[vmem] * 3 + [hbm] * 5,
        out_specs=(vmem, vmem, hbm, hbm),
        scratch_shapes=scratch,
        compiler_params=pltpu.CompilerParams(
            collective_id=0, has_side_effects=True, vmem_limit_bytes=56 * 2**20
        ),
        name="layer",
    )(
        token_adapter_index.reshape(1, -1),
        tokens,
        cotangent,
        gate,
        up,
        down,
        imaps.reshape(adapters * rank, width),
        omaps.reshape(adapters * rank, hidden),
    )
    return (
        ref_out,
        pol_out,
        in_grad.reshape(adapters, rank, width),
        out_grad.reshape(adapters, rank, hidden),
    )


def solution(mesh):
    in_specs = (
        P("fsdp", "tp"),
        P(),
        P("tp", "fsdp"),
        P("tp", "fsdp"),
        P("fsdp", "tp"),
        P(None, None, "tp"),
        P(None, None, "fsdp"),
        P("fsdp", "tp"),
    )
    out_specs = (P("fsdp", "tp"), P("fsdp", "tp"), P(None, None, "tp"), P(None, None, "fsdp"))
    return jax.shard_map(body, mesh=mesh, in_specs=in_specs, out_specs=out_specs, check_vma=False)
```

time: 897 us -> 81.4 us (0.09); the launches traced: 882 us -> 81 us
  blocking collectives: 584 us -> 0 us
  waiting for transfers between devices: 258 us -> 0 us
  Pallas kernels: 0 us -> 73.8 us
  between operations: 14.6 us -> 0.64 us
  matrix products: 13.4 us -> 0 us
    unnamed x1 -> x0, blocking collectives: 399 us -> none
    all_gather x2 -> x0, waiting for transfers between devices: 229 us -> none  [the longest x1 118 us: body(): collected_rows = lax.all_gather(tokens, 'fsdp', axis=0, tiled=True)]
    all_gather x1 -> x0, blocking collectives: 174 us -> none  [body(): lax.all_gather(backward_share.astype(jnp.bfloat16), 'fsdp', axis=0, tiled...]
    pallas_call x0 -> x1, Pallas kernels: none -> 73.8 us  [body(): pl.pallas_call(kernel, out_shape=(jax.ShapeDtypeStruct((4, width), BF), j...]
    psum x1 -> x0, waiting for transfers between devices: 27.8 us -> none  [body(): lax.psum((gate_piece, up_piece, adapter_piece), 'tp')]
    dot_general x9 -> x0, matrix products: 13.4 us -> none  [the longest x3 4.16 us: contract_trailing(): lax.dot_general(left, right, (((1,), (1,)), ((), ())), preferred_element_...]
    psum x1 -> x0, blocking collectives: 11.7 us -> none  [body(): lax.psum((gate_piece, up_piece, adapter_piece), 'tp')]
  transfers between devices with their start and end apart: 3 -> 0, of which waited for: 3 -> 0; matrix products, arithmetic and copies ran while one was open for 1% -> 0% of each run, Pallas kernels for 0% -> 0%
where the time goes in v1:
time: 81.4 us; the launch traced here: 81 us
  Pallas kernels  73.8 us (91%)
  local copies, waits for them, and re-layouts  6.54 us (8%)
    pallas_call x1, Pallas kernels, body(): pl.pallas_call(kernel, out_shape=(jax.ShapeDtypeStruct((4, width), BF), j...  73.8 us
    unnamed x6, local copies, waits for them, and re-layouts  6.54 us

profile of v1, /device:TPU:32, one launch (start us, length us, event | category | flops | bytes accessed | tf_op | source)
XLA Modules:
  0.0 81.0 jit_solution(1142377187737311934)
XLA Ops:
  0.6 73.8 %layer.1 = (bf16[4,2048]{1,0:T(4,128)(2,1)}, bf16[4,2048]{1,0:T(4,128)(2,1)}, f32[256,2048]{1,0:T(8,128)}, f32[256,256]{1,0:T(8,128)}) custom-call(s32[1,256]{1,0:T(1,128)} %bitcast.9, bf16[4,2048]{1,0:T(4,128)(2,1)} %tok.1, bf16[4,2048]{1,0:T(4,128)(2,1)} %cot.1, bf16[2048,256]{1,0:T(8,128)(2,1)} %gate.1, bf16[2048,256]{1,0:T(8,128)(2,1)} %up.1, ...), custom_call_target="tpu_custom_call" | custom-call | tf_op jit(solution)/shard_map/layer/pallas_call | solution.py:361
  74.4 1.3 %copy.16 = bf16[4,2048]{1,0:T(4,128)(2,1)} copy(bf16[4,2048]{1,0:T(4,128)(2,1)} %get-tuple-element.16) | data formatting | bytes 32768
  75.7 1.3 %copy.17 = bf16[4,2048]{1,0:T(4,128)(2,1)} copy(bf16[4,2048]{1,0:T(4,128)(2,1)} %get-tuple-element.17) | data formatting | bytes 32768
  77.1 0.0 copy-start
  77.1 3.2 %copy.18 = f32[4,64,2048]{2,1,0:T(8,128)} copy(f32[4,64,2048]{2,1,0:T(8,128)} %bitcast.5) | data formatting | bytes 4194304
  80.3 0.0 copy-done
  80.3 0.7 copy.19
Async XLA Ops:
  77.1 3.2 %copy-start = (f32[256,256]{1,0:T(8,128)S(1)}, f32[256,256]{1,0:T(8,128)}, u32[]{:S(2)}) copy-start(f32[256,256]{1,0:T(8,128)} %get-tuple-element.11) | copy-start | bytes 786436

commit v2 on v1

--- a/solution.py
+++ b/solution.py
@@ -11,7 +11,7 @@
 BF = jnp.bfloat16
 F32 = jnp.float32
 
-GROUPS = (("z", 0, 512), ("p", 512, 768), ("p", 1280, 768))
+GROUPS = (("z", 0, 768), ("p", 768, 512), ("p", 1280, 768))
 
 
 def nt(a, b):
@@ -39,19 +39,18 @@
 
 def kernel(
     idx, tok, cot, gate, up, down, imaps, omaps,
-    ref_out, pol_out, in_grad, out_grad,
+    ref_out, pol_out, back_out, xt_out, wide_out, gup_out,
     gate_v, up_v, down_v, imaps_v, omaps_v,
     ta, tb, ca, cb, xt, ct,
     f1, s1, r1, s2, r2, e1, er1,
     f2, g1, gr1, g2, gr2, e2, er2,
     act_v, mask_v, lw_v, href, hpol, gup, hrp, hpp,
     ar0, ar1, ar1s, ar2, ar2s, ar3,
-    in_v, out_v,
     *rest,
 ):
     ngroups = len(GROUPS)
     ysend, yrecv, zsend, zrecv = (rest[i * ngroups : (i + 1) * ngroups] for i in range(4))
-    wsem, ssem, rsem, osem = rest[4 * ngroups :]
+    relay3, relay4, acc, wsem, ssem, rsem, osem = rest[4 * ngroups :]
 
     f = lax.axis_index("fsdp")
     t = lax.axis_index("tp")
@@ -173,6 +172,8 @@
 
     finish(second_t, far_t)
     unpack(ta, tb, xt)
+    xt_copy = pltpu.make_async_copy(xt, xt_out, osem.at[0])
+    xt_copy.start()
     for load in loads[:3]:
         load.wait()
     f1[:, 0:256] = nn(xt[...], gate_v[...])
@@ -186,10 +187,10 @@
     s1[...] = f1[other, :].astype(BF)
     core_t = send(s1, r1, tdev(1))
     far_c = third_hops(ca, second_c)
+
     core_t.wait_recv()
     s2[...] = (f1[own, :] + r1[...].astype(F32)).astype(BF)
     line_t = send(s2, r2, tdev(2))
-
     finish(second_c, far_c)
     unpack(ca, cb, ct)
     for load in loads[3:]:
@@ -227,22 +228,30 @@
     hpp[...] = nn(plane_major, hpol[...]).astype(BF)
 
     stage1 = []
-    for n, (kind, start, width) in enumerate(GROUPS):
+
+    def first_stage(n):
+        kind, start, width = GROUPS[n]
         pair = (href, hpol) if kind == "z" else (hrp, hpp)
+        half = width // 2
         for o in range(2):
             for q in range(2):
-                half = width // 2
                 block = nn(pair[o][...], down_v[:, start + q * half : start + (q + 1) * half]).astype(BF)
                 ysend[n][:, o, :, q * half : (q + 1) * half] = block.reshape(8, 32, half)
-        me = z if kind == "z" else p
         copies = []
-        for k in range(1, 8):
-            to = lax.rem(z + k, 8) if kind == "z" else pidx(k)
-            copies.append(
-                send(ysend[n].at[to], yrecv[n].at[me], zdev(k) if kind == "z" else pdev(k))
-            )
-        yrecv[n][me] = ysend[n][me]
+        if kind == "z":
+            for m, sign in ((0, 1), (1, -1)):
+                copies.append(send(ysend[n].at[lax.rem(z + 3 * sign + 8, 8)], relay3.at[m], zdev(sign)))
+                copies.append(send(ysend[n].at[lax.rem(z + 4, 8), m], relay4.at[m], zdev(2 * sign)))
+            for m, sign in ((0, 1), (1, -1)):
+                copies.append(send(ysend[n].at[lax.rem(z + sign + 8, 8)], yrecv[n].at[m], zdev(sign)))
+        else:
+            for k in range(1, 8):
+                copies.append(send(ysend[n].at[pidx(k)], yrecv[n].at[p], pdev(k)))
+            yrecv[n][p] = ysend[n][p]
         stage1.append(copies)
+
+    first_stage(0)
+    first_stage(1)
 
     line_c.wait_recv()
     grad = g2[...].astype(F32) + gr2[...].astype(F32)
@@ -252,35 +261,40 @@
     pair_c.wait_recv()
     gup[other, :] = er2[...]
 
+    wide_copy = pltpu.make_async_copy(lw_v, wide_out, osem.at[1])
+    wide_copy.start()
+    gup_copy = pltpu.make_async_copy(gup, gup_out, osem.at[2])
+    gup_copy.start()
     mine = pl.ds(pl.multiple_of(t * 64, 64), 64)
     back = (nt(gup[mine, :], omaps_v[...]) * mask_v[mine, :].astype(F32)).astype(BF)
     ar0[...] = (nn(back[:32], fold_lo) + nn(back[32:], fold_hi)).astype(BF)
     ar1[p] = ar0[...]
     sum1 = [send(ar0, ar1.at[p], pdev(k)) for k in range(1, 8)]
-    out_v[...] = tn(lw_v[...], gup[...])
-    out_copy = pltpu.make_async_copy(out_v, out_grad, osem.at[0])
-    out_copy.start()
-    for copy in sum1:
-        copy.wait_recv()
-    ar1s[...] = jnp.sum(ar1[...].astype(F32), axis=0).astype(BF)
-    ar2[z] = ar1s[...]
-    sum2 = [send(ar1s, ar2.at[z], zdev(k)) for k in range(1, 8)]
-    for copy in sum2:
-        copy.wait_recv()
-    ar2s[...] = jnp.sum(ar2[...].astype(F32), axis=0).astype(BF)
-    ar3[t] = ar2s[...]
-    sum3 = [send(ar2s, ar3.at[t], tdev(k)) for k in range(1, 4)]
+
+    first_stage(2)
+    for n in range(4):
+        stage1[0][n].wait_recv()
+    for m, sign in ((0, 1), (1, -1)):
+        block = ysend[0][lax.rem(z + 2 * sign + 8, 8)].astype(F32) + relay3[m].astype(F32)
+        acc[m, m] = (block[m] + relay4[m].astype(F32)).astype(BF)
+        acc[m, 1 - m] = block[1 - m].astype(BF)
+        stage1[0].append(send(acc.at[m], yrecv[0].at[2 + m], zdev(2 * sign)))
 
     stage2 = []
-    for n, (kind, start, width) in enumerate(GROUPS):
+
+    def second_stage(n):
+        kind, start, width = GROUPS[n]
         half = width // 2
-        for copy in stage1[n]:
+        for copy in stage1[n][4:] if kind == "z" else stage1[n]:
             copy.wait_recv()
         pieces = []
         for q in range(2):
             for o in range(2):
-                piece = yrecv[n][:, o, :, q * half : (q + 1) * half].astype(F32)
-                pieces.append(jnp.sum(piece, axis=0).astype(BF))
+                columns = slice(q * half, (q + 1) * half)
+                piece = jnp.sum(yrecv[n][:, o, :, columns].astype(F32), axis=0)
+                if kind == "z":
+                    piece = piece + ysend[n][z, o, :, columns].astype(F32)
+                pieces.append(piece.astype(BF))
         stacked = jnp.concatenate(pieces, axis=0)
         zsend[n][...] = nn(regroup, stacked).astype(BF).reshape(8, 16, half)
         me = p if kind == "z" else z
@@ -293,21 +307,26 @@
         zrecv[n][me] = zsend[n][me]
         stage2.append(copies)
 
+    for copy in sum1:
+        copy.wait_recv()
+    ar1s[...] = jnp.sum(ar1[...].astype(F32), axis=0).astype(BF)
+    ar2[z] = ar1s[...]
+    sum2 = [send(ar1s, ar2.at[z], zdev(k)) for k in range(1, 8)]
+    second_stage(0)
+    second_stage(1)
+    for copy in sum2:
+        copy.wait_recv()
+    ar2s[...] = jnp.sum(ar2[...].astype(F32), axis=0).astype(BF)
+    ar3[t] = ar2s[...]
+    sum3 = [send(ar2s, ar3.at[t], tdev(k)) for k in range(1, 4)]
+    second_stage(2)
     for copy in sum3:
         copy.wait_recv()
     wides = []
     for k in range(4):
         for fold in (fold_lo, fold_hi):
             wides.append(nt(ar3[k], fold))
-    back_wide = (jnp.concatenate(wides, axis=0) * mask_v[...].astype(F32)).astype(BF)
-    in_copies = []
-    for k in range(4):
-        in_v[:, k * 512 : (k + 1) * 512] = tn(back_wide, xt[:, k * 512 : (k + 1) * 512])
-        copy = pltpu.make_async_copy(
-            in_v.at[:, pl.ds(k * 512, 512)], in_grad.at[:, pl.ds(k * 512, 512)], osem.at[1 + k]
-        )
-        copy.start()
-        in_copies.append(copy)
+    back_out[...] = (jnp.concatenate(wides, axis=0) * mask_v[...].astype(F32)).astype(BF)
 
     i4, j16 = iota2(4, 16)
     for n, (kind, start, width) in enumerate(GROUPS):
@@ -320,14 +339,46 @@
                 pick = as_matrix(j16 == o * 8 + q * 4 + i4)
                 out[:, start + q * half : start + (q + 1) * half] = nn(pick, total).astype(BF)
 
-    out_copy.wait()
-    for copy in in_copies:
+    for copy in (xt_copy, wide_copy, gup_copy):
         copy.wait()
     for copy in pending:
         copy.wait_send()
 
 
-COPIES = 2 * (14 + 11 + 4) + 6 + 17 + 14 * len(GROUPS)
+def gradients(
+    ref_in, pol_in, back, wide, gup, xt, ref_out, pol_out, in_grad, out_grad,
+    rv, pv, bv, wv, uv, xv, gv, ov, isem, osem,
+):
+    sources = [back, wide, gup, ref_in, pol_in] + [xt.at[:, pl.ds(k * 512, 512)] for k in range(4)]
+    places = [bv, wv, uv, rv, pv] + [xv.at[k] for k in range(4)]
+    loads = []
+    for n in range(9):
+        load = pltpu.make_async_copy(sources[n], places[n], isem.at[n])
+        load.start()
+        loads.append(load)
+    stores = []
+
+    def store(src, dst):
+        copy = pltpu.make_async_copy(src, dst, osem.at[len(stores)])
+        copy.start()
+        stores.append(copy)
+
+    loads[0].wait()
+    for k in range(4):
+        loads[5 + k].wait()
+        gv[k] = tn(bv[...], xv[k])
+        store(gv.at[k], in_grad.at[:, pl.ds(k * 512, 512)])
+    for n in (1, 2, 3, 4):
+        loads[n].wait()
+    store(rv, ref_out)
+    store(pv, pol_out)
+    ov[...] = tn(wv[...], uv[...])
+    store(ov, out_grad)
+    for copy in stores:
+        copy.wait()
+
+
+COPIES = 2 * (14 + 11 + 4) + 6 + 17 + 14 * len(GROUPS) + 1
 
 
 def body(tokens, token_adapter_index, gate, up, down, imaps, omaps, cotangent):
@@ -348,26 +399,30 @@
         v((256, 256), BF), v((256, 256), BF), v((256, 256), BF),
         v((32, 128), BF), v((8, 32, 128), BF), v((32, 128), BF), v((8, 32, 128), BF), v((32, 128), BF),
         v((4, 32, 128), BF),
-        v((256, 2048), F32), v((256, 256), F32),
     ]
-    scratch += [v((8, 2, 32, w), BF) for _, _, w in GROUPS] * 2
+    scratch += [v((8, 2, 32, w), BF) for _, _, w in GROUPS]
+    scratch += [v((4 if kind == "z" else 8, 2, 32, w), BF) for kind, _, w in GROUPS]
     scratch += [v((8, 16, w // 2), BF) for _, _, w in GROUPS] * 2
+    first = GROUPS[0][2]
+    scratch += [v((2, 2, 32, first), BF), v((2, 32, first), BF), v((2, 2, 32, first), BF)]
     scratch += [
         pltpu.SemaphoreType.DMA((5,)),
         pltpu.SemaphoreType.DMA((COPIES,)),
         pltpu.SemaphoreType.DMA((COPIES,)),
-        pltpu.SemaphoreType.DMA((5,)),
+        pltpu.SemaphoreType.DMA((3,)),
     ]
-    ref_out, pol_out, in_grad, out_grad = pl.pallas_call(
+    ref_out, pol_out, back, xt, wide, gup = pl.pallas_call(
         kernel,
         out_shape=(
             jax.ShapeDtypeStruct((4, width), BF),
             jax.ShapeDtypeStruct((4, width), BF),
-            jax.ShapeDtypeStruct((adapters * rank, width), F32),
-            jax.ShapeDtypeStruct((adapters * rank, hidden), F32),
+            jax.ShapeDtypeStruct((256, 256), BF),
+            jax.ShapeDtypeStruct((256, width), BF),
+            jax.ShapeDtypeStruct((256, 256), BF),
+            jax.ShapeDtypeStruct((256, 256), BF),
         ),
         in_specs=[vmem] * 3 + [hbm] * 5,
-        out_specs=(vmem, vmem, hbm, hbm),
+        out_specs=(vmem, vmem, vmem, hbm, hbm, hbm),
         scratch_shapes=scratch,
         compiler_params=pltpu.CompilerParams(
             collective_id=0, has_side_effects=True, vmem_limit_bytes=56 * 2**20
@@ -383,6 +438,24 @@
         imaps.reshape(adapters * rank, width),
         omaps.reshape(adapters * rank, hidden),
     )
+    ref_out, pol_out, in_grad, out_grad = pl.pallas_call(
+        gradients,
+        out_shape=(
+            jax.ShapeDtypeStruct((4, width), BF),
+            jax.ShapeDtypeStruct((4, width), BF),
+            jax.ShapeDtypeStruct((adapters * rank, width), F32),
+            jax.ShapeDtypeStruct((adapters * rank, hidden), F32),
+        ),
+        in_specs=[hbm] * 6,
+        out_specs=(hbm,) * 4,
+        scratch_shapes=[
+            v((4, width), BF), v((4, width), BF), v((256, 256), BF), v((256, 256), BF), v((256, 256), BF),
+            v((4, 256, 512), BF), v((4, 256, 512), F32), v((256, 256), F32),
+            pltpu.SemaphoreType.DMA((9,)), pltpu.SemaphoreType.DMA((7,)),
+        ],
+        compiler_params=pltpu.CompilerParams(vmem_limit_bytes=60 * 2**20),
+        name="gradients",
+    )(ref_out, pol_out, back, wide, gup, xt)
     return (
         ref_out,
         pol_out,

time: 81.4 us -> 69 us (0.85)
  local copies, waits for them, and re-layouts: 6.54 us -> 0 us
  Pallas kernels: 73.8 us -> 67.5 us
    pallas_call x1, Pallas kernels: 73.8 us -> 64.2 us  [body(): pl.pallas_call(kernel, out_shape=(jax.ShapeDtypeStruct((4, width), BF), j...]
    unnamed x6 -> x0, local copies, waits for them, and re-layouts: 6.54 us -> none
    pallas_call x0 -> x1, Pallas kernels: none -> 3.3 us  [body(): pl.pallas_call(gradients, out_shape=(jax.ShapeDtypeStruct((4, width), BF)...]
where the time goes in v2:
time: 69 us; the launch traced here: 68.1 us
  Pallas kernels  67.5 us (98%)
    pallas_call x1, Pallas kernels, body(): pl.pallas_call(kernel, out_shape=(jax.ShapeDtypeStruct((4, width), BF), j...  64.2 us
    pallas_call x1, Pallas kernels, body(): pl.pallas_call(gradients, out_shape=(jax.ShapeDtypeStruct((4, width), BF)...  3.3 us

profile of v2, /device:TPU:32, one launch (start us, length us, event | category | flops | bytes accessed | tf_op | source)
XLA Modules:
  0.0 68.1 jit_solution(4099460007769833995)
XLA Ops:
  0.6 64.2 %layer.1 = (bf16[4,2048]{1,0:T(4,128)(2,1)}, bf16[4,2048]{1,0:T(4,128)(2,1)}, bf16[256,256]{1,0:T(8,128)(2,1)}, bf16[256,2048]{1,0:T(8,128)(2,1)}, bf16[256,256]{1,0:T(8,128)(2,1)}, /*index=5*/bf16[256,256]{1,0:T(8,128)(2,1)}) custom-call(s32[1,256]{1,0:T(1,128)} %bitcast.7, bf16[4,2048]{1,0:T(4,128)(2,1)} %tok.1, bf16[4,2048]{1,0:T(4,128)(2,1)} %cot.1, ...), custom_call_target="tpu_custom_call" | custom-call | tf_op jit(solution)/shard_map/layer/pallas_call | solution.py:414
  64.8 3.3 %gradients.1 = (bf16[4,2048]{1,0:T(4,128)(2,1)}, bf16[4,2048]{1,0:T(4,128)(2,1)}, f32[256,2048]{1,0:T(8,128)}, f32[256,256]{1,0:T(8,128)}) custom-call(bf16[4,2048]{1,0:T(4,128)(2,1)} %get-tuple-element.14.ref_in, bf16[4,2048]{1,0:T(4,128)(2,1)} %get-tuple-element.15.pol_in, bf16[256,256]{1,0:T(8,128)(2,1)} %get-tuple-element.16.back, ...), custom_call_target="tpu_custom_call" | custom-call | tf_op jit(solution)/shard_map/gradients/pallas_call | solution.py:441

commit v3 on v2

--- a/solution.py
+++ b/solution.py
@@ -11,7 +11,11 @@
 BF = jnp.bfloat16
 F32 = jnp.float32
 
-GROUPS = (("z", 0, 768), ("p", 768, 512), ("p", 1280, 768))
+GROUPS = (("z", 0, 1024), ("p", 1024, 512), ("p", 1536, 512))
+
+
+Z_STEPS = (4, 3, 5, 2, 6, 1, 7)
+P_STEPS = (5, 3, 7, 1, 4, 2, 6)
 
 
 def nt(a, b):
@@ -91,7 +95,7 @@
         loads.append(load)
 
     barrier = pltpu.get_barrier_semaphore()
-    partners = [zdev(k) for k in range(1, 8)] + [pdev(k) for k in range(1, 8)] + [tdev(k) for k in range(1, 4)]
+    partners = [zdev(k) for k in Z_STEPS] + [pdev(k) for k in P_STEPS] + [tdev(k) for k in range(1, 4)]
     for device in partners:
         pl.semaphore_signal(barrier, 1, device_id=device, device_id_type=MESH)
 
@@ -107,28 +111,25 @@
         half_b[z, p] = packed[:, 256:]
 
     i8, j8 = iota2(8, 256)
+    i256, j256 = iota2(256, 256)
     chosen = as_matrix(idx[...] == i8)
-    mask_v[...] = tn(chosen, as_matrix(i8 == j8 // 64)).astype(BF)
+    order = as_matrix(j256 == ((i256 // 2) % 64) * 4 + (i256 // 128) * 2 + i256 % 2)
+    mask_v[...] = nn(order, tn(chosen, as_matrix(i8 == j8 // 64)).astype(BF)).astype(BF)
 
     pl.semaphore_wait(barrier, len(partners))
 
     def first_hops(half_a, half_b):
-        a = [send(half_a.at[z, p], half_a.at[z, p], pdev(k)) for k in range(1, 8)]
-        b = [send(half_b.at[z, p], half_b.at[z, p], zdev(k)) for k in range(1, 8)]
+        a = [send(half_a.at[z, p], half_a.at[z, p], pdev(k)) for k in P_STEPS]
+        b = [send(half_b.at[z, p], half_b.at[z, p], zdev(k)) for k in Z_STEPS]
         return a, b
 
-    def second_hops(half_a, half_b, first):
-        a, b = first
-        for copy in a:
-            copy.wait_recv()
-        near = [send(half_a.at[z], half_a.at[z], zdev(k)) for k in (2, -2, 1, -1)]
-        for copy in b:
-            copy.wait_recv()
-        plane = [send(half_b.at[:, p], half_b.at[:, p], pdev(k)) for k in range(1, 8)]
-        return near, plane
-
-    def third_hops(half_a, second):
-        near, _ = second
+    def near_hops(half_a):
+        return [send(half_a.at[z], half_a.at[z], zdev(k)) for k in (2, -2, 1, -1)]
+
+    def plane_hops(half_b):
+        return [send(half_b.at[:, p], half_b.at[:, p], pdev(k)) for k in P_STEPS]
+
+    def far_hops(half_a, near):
         far = []
         for n, sign in ((0, 1), (1, -1)):
             near[n].wait_recv()
@@ -138,168 +139,187 @@
             far.append(send(half_a.at[block], half_a.at[block], zdev(sign)))
         return far
 
-    def finish(second, far):
-        near, plane = second
-        for copy in near[2:] + plane + far:
+    def arrived(copies):
+        for copy in copies:
             copy.wait_recv()
 
     first_t = first_hops(ta, tb)
     first_c = first_hops(ca, cb)
-    second_t = second_hops(ta, tb, first_t)
-    far_t = third_hops(ta, second_t)
-    second_c = second_hops(ca, cb, first_c)
-
-    i256, j256 = iota2(256, 256)
-    spread16 = as_matrix(j256 == ((i256 // 4) % 16) * 16 + (i256 // 64) * 4 + i256 % 4)
-    plane_major = as_matrix(j256 == ((i256 // 4) % 8) * 32 + (i256 // 32) * 4 + i256 % 4)
+    arrived(first_t[0])
+    near_t = near_hops(ta)
+    arrived(first_t[1])
+    plane_t = plane_hops(tb)
+
+    spread16 = as_matrix(
+        j256 == ((i256 // 2) % 16) * 16 + (i256 // 64) * 4 + ((i256 // 32) % 2) * 2 + i256 % 2
+    )
+    i128, j128 = iota2(128, 128)
+    plane_major = as_matrix(j128 == ((i128 // 2) % 8) * 16 + (i128 // 16) * 2 + i128 % 2)
     ifold, jfold = iota2(256, 128)
     fold_lo = as_matrix(ifold % 64 == jfold)
     fold_hi = as_matrix(ifold % 64 + 64 == jfold)
-    i128, j128 = iota2(128, 128)
     regroup = as_matrix(
-        j128 == ((i128 // 4) % 2) * 64 + ((i128 // 8) % 2) * 32 + (i128 // 16) * 4 + i128 % 4
+        j128
+        == ((i128 // 4) % 2) * 64 + ((i128 // 8) % 2) * 32 + ((i128 // 2) % 2) * 16 + (i128 // 16) * 2 + i128 % 2
     )
 
-    def unpack(half_a, half_b, whole):
+    far_t = far_hops(ta, near_t)
+    arrived(first_c[0])
+    near_c = near_hops(ca)
+    arrived(first_c[1])
+    plane_c = plane_hops(cb)
+
+    def unpack(half, n, whole):
         for g in range(4):
-            for n, half in enumerate((half_a, half_b)):
-                block = half[2 * g : 2 * g + 2].reshape(256, 256)
-                rows = nn(spread16, block).astype(BF)
-                for q in range(4):
-                    whole[g * 64 : (g + 1) * 64, q * 512 + n * 256 : q * 512 + (n + 1) * 256] = rows[
-                        q * 64 : (q + 1) * 64
-                    ]
-
-    finish(second_t, far_t)
-    unpack(ta, tb, xt)
-    xt_copy = pltpu.make_async_copy(xt, xt_out, osem.at[0])
-    xt_copy.start()
+            block = nn(spread16, half[2 * g : 2 * g + 2].reshape(256, 256)).astype(BF)
+            for q in range(4):
+                for j in range(2):
+                    whole[j * 128 + g * 32 : j * 128 + (g + 1) * 32, q * 512 + n * 256 : q * 512 + (n + 1) * 256] = (
+                        block[q * 64 + j * 32 : q * 64 + (j + 1) * 32]
+                    )
+
+    rows = [slice(j * 128, (j + 1) * 128) for j in range(2)]
+    own = [pl.ds(pl.multiple_of(j * 128 + c * 64, 64), 64) for j in range(2)]
+    other = [pl.ds(pl.multiple_of(j * 128 + (1 - c) * 64, 64), 64) for j in range(2)]
+
+    def to_line(j, copy):
+        copy.wait_recv()
+        s2[j] = (f1[own[j], :] + r1[j].astype(F32)).astype(BF)
+        return send(s2.at[j], r2.at[j], tdev(2))
+
+    arrived(plane_t)
+    unpack(tb, 1, xt)
     for load in loads[:3]:
         load.wait()
+    arrived(near_t[2:] + far_t)
+    unpack(ta, 0, xt)
     f1[:, 0:256] = nn(xt[...], gate_v[...])
     f1[:, 256:512] = nn(xt[...], up_v[...])
     low = (nt(xt[...], imaps_v[...]) * mask_v[...].astype(F32)).astype(BF)
     f1[:, 512:640] = nn(low, fold_lo)
-
-    own = pl.ds(pl.multiple_of(c * 128, 128), 128)
-    other = pl.ds(pl.multiple_of((1 - c) * 128, 128), 128)
-
-    s1[...] = f1[other, :].astype(BF)
-    core_t = send(s1, r1, tdev(1))
-    far_c = third_hops(ca, second_c)
-
-    core_t.wait_recv()
-    s2[...] = (f1[own, :] + r1[...].astype(F32)).astype(BF)
-    line_t = send(s2, r2, tdev(2))
-    finish(second_c, far_c)
-    unpack(ca, cb, ct)
+    core_t = []
+    for j in range(2):
+        s1[j] = f1[other[j], :].astype(BF)
+        core_t.append(send(s1.at[j], r1.at[j], tdev(1)))
+    xt_copy = pltpu.make_async_copy(xt, xt_out, osem.at[0])
+    xt_copy.start()
+    line_0 = to_line(0, core_t[0])
+    line_1 = to_line(1, core_t[1])
+    far_c = far_hops(ca, near_c)
+
     for load in loads[3:]:
         load.wait()
-    f2[...] = nt(ct[...], down_v[...])
-    g1[...] = f2[other, :].astype(BF)
-    core_c = send(g1, gr1, tdev(1))
-
-    line_t.wait_recv()
-    total = s2[...].astype(F32) + r2[...].astype(F32)
-    gate_values = total[:, 0:256]
-    up_values = total[:, 256:512]
-    lora_in = total[:, 512:640].astype(BF)
-    wide = (nt(lora_in, fold_lo) * mask_v[own, :].astype(F32)).astype(BF)
-    activated = gate_values / (1.0 + jnp.exp(-gate_values))
-    act_v[...] = activated
-    up_policy = up_values + nn(wide, omaps_v[...])
-    e1[:, 0:256] = (activated * up_values).astype(BF)
-    e1[:, 256:512] = (activated * up_policy).astype(BF)
-    e1[:, 512:640] = lora_in
-    pair_t = send(e1, er1, tdev(1))
-
-    core_c.wait_recv()
-    g2[...] = (f2[own, :] + gr1[...].astype(F32)).astype(BF)
-    line_c = send(g2, gr2, tdev(2))
-
-    href[own, :] = e1[:, 0:256]
-    hpol[own, :] = e1[:, 256:512]
-    lw_v[own, :] = wide
-    pair_t.wait_recv()
-    href[other, :] = er1[:, 0:256]
-    hpol[other, :] = er1[:, 256:512]
-    lw_v[other, :] = (nt(er1[:, 512:640], fold_lo) * mask_v[other, :].astype(F32)).astype(BF)
-    hrp[...] = nn(plane_major, href[...]).astype(BF)
-    hpp[...] = nn(plane_major, hpol[...]).astype(BF)
-
-    stage1 = []
-
-    def first_stage(n):
+
+    def activate(j, copy):
+        copy.wait_recv()
+        total = s2[j].astype(F32) + r2[j].astype(F32)
+        gate_values = total[:, 0:256]
+        up_values = total[:, 256:512]
+        lora_in = total[:, 512:640].astype(BF)
+        wide = (nt(lora_in, fold_lo) * mask_v[own[j], :].astype(F32)).astype(BF)
+        activated = gate_values / (1.0 + jnp.exp(-gate_values))
+        act_v[j] = activated
+        up_policy = up_values + nn(wide, omaps_v[...])
+        e1[j, :, 0:256] = (activated * up_values).astype(BF)
+        e1[j, :, 256:512] = (activated * up_policy).astype(BF)
+        e1[j, :, 512:640] = lora_in
+        pair = send(e1.at[j], er1.at[j], tdev(1))
+        href[own[j], :] = e1[j, :, 0:256]
+        hpol[own[j], :] = e1[j, :, 256:512]
+        lw_v[own[j], :] = wide
+        return pair
+
+    def collect(j, copy):
+        copy.wait_recv()
+        href[other[j], :] = er1[j, :, 0:256]
+        hpol[other[j], :] = er1[j, :, 256:512]
+        lw_v[other[j], :] = (nt(er1[j, :, 512:640], fold_lo) * mask_v[other[j], :].astype(F32)).astype(BF)
+        hrp[rows[j], :] = nn(plane_major, href[rows[j], :]).astype(BF)
+        hpp[rows[j], :] = nn(plane_major, hpol[rows[j], :]).astype(BF)
+
+    stage1 = [[[], []] for _ in GROUPS]
+
+    def first_stage(n, j):
         kind, start, width = GROUPS[n]
         pair = (href, hpol) if kind == "z" else (hrp, hpp)
         half = width // 2
         for o in range(2):
             for q in range(2):
-                block = nn(pair[o][...], down_v[:, start + q * half : start + (q + 1) * half]).astype(BF)
-                ysend[n][:, o, :, q * half : (q + 1) * half] = block.reshape(8, 32, half)
-        copies = []
+                block = nn(pair[o][rows[j], :], down_v[:, start + q * half : start + (q + 1) * half]).astype(BF)
+                ysend[n][j, :, o, :, q * half : (q + 1) * half] = block.reshape(8, 16, half)
+        copies = stage1[n][j]
         if kind == "z":
             for m, sign in ((0, 1), (1, -1)):
-                copies.append(send(ysend[n].at[lax.rem(z + 3 * sign + 8, 8)], relay3.at[m], zdev(sign)))
-                copies.append(send(ysend[n].at[lax.rem(z + 4, 8), m], relay4.at[m], zdev(2 * sign)))
+                copies.append(send(ysend[n].at[j, lax.rem(z + 3 * sign + 8, 8)], relay3.at[j, m], zdev(sign)))
+                copies.append(send(ysend[n].at[j, lax.rem(z + 4, 8), m], relay4.at[j, m], zdev(2 * sign)))
             for m, sign in ((0, 1), (1, -1)):
-                copies.append(send(ysend[n].at[lax.rem(z + sign + 8, 8)], yrecv[n].at[m], zdev(sign)))
+                copies.append(send(ysend[n].at[j, lax.rem(z + sign + 8, 8)], yrecv[n].at[j, m], zdev(sign)))
         else:
-            for k in range(1, 8):
-                copies.append(send(ysend[n].at[pidx(k)], yrecv[n].at[p], pdev(k)))
-            yrecv[n][p] = ysend[n][p]
-        stage1.append(copies)
-
-    first_stage(0)
-    first_stage(1)
-
+            for k in P_STEPS:
+                copies.append(send(ysend[n].at[j, pidx(k)], yrecv[n].at[j, p], pdev(k)))
+            yrecv[n][j, p] = ysend[n][j, p]
+
+    def relay(j):
+        arrived(stage1[0][j][:4])
+        for m, sign in ((0, 1), (1, -1)):
+            block = ysend[0][j, lax.rem(z + 2 * sign + 8, 8)].astype(F32) + relay3[j, m].astype(F32)
+            acc[j, m, m] = (block[m] + relay4[j, m].astype(F32)).astype(BF)
+            acc[j, m, 1 - m] = block[1 - m].astype(BF)
+            stage1[0][j].append(send(acc.at[j, m], yrecv[0].at[j, 2 + m], zdev(2 * sign)))
+
+    pair_0 = activate(0, line_0)
+    pair_1 = activate(1, line_1)
+    arrived(near_c[2:] + plane_c + far_c)
+    unpack(ca, 0, ct)
+    unpack(cb, 1, ct)
+    f2[...] = nt(ct[...], down_v[...])
+    for j in range(2):
+        g1[j] = f2[other[j], :].astype(BF)
+    core_c = send(g1, gr1, tdev(1))
+    collect(0, pair_0)
+    first_stage(0, 0)
+    core_c.wait_recv()
+    for j in range(2):
+        g2[j] = (f2[own[j], :] + gr1[j].astype(F32)).astype(BF)
+    line_c = send(g2, gr2, tdev(2))
+    first_stage(1, 0)
+    collect(1, pair_1)
+    first_stage(0, 1)
+    relay(0)
+    first_stage(1, 1)
     line_c.wait_recv()
-    grad = g2[...].astype(F32) + gr2[...].astype(F32)
-    e2[...] = (grad * act_v[...]).astype(BF)
+    e2[...] = ((g2[...].astype(F32) + gr2[...].astype(F32)) * act_v[...]).astype(BF)
+    mine = pl.ds(pl.multiple_of(t * 64, 64), 64)
+    back = (nt(e2[t // 2], omaps_v[...]) * mask_v[mine, :].astype(F32)).astype(BF)
+    ar0[...] = (nn(back[:32], fold_lo) + nn(back[32:], fold_hi)).astype(BF)
+    sum1 = [send(ar0, ar1.at[p], pdev(k)) for k in P_STEPS]
     pair_c = send(e2, er2, tdev(1))
-    gup[own, :] = e2[...]
-    pair_c.wait_recv()
-    gup[other, :] = er2[...]
-
-    wide_copy = pltpu.make_async_copy(lw_v, wide_out, osem.at[1])
-    wide_copy.start()
-    gup_copy = pltpu.make_async_copy(gup, gup_out, osem.at[2])
-    gup_copy.start()
-    mine = pl.ds(pl.multiple_of(t * 64, 64), 64)
-    back = (nt(gup[mine, :], omaps_v[...]) * mask_v[mine, :].astype(F32)).astype(BF)
-    ar0[...] = (nn(back[:32], fold_lo) + nn(back[32:], fold_hi)).astype(BF)
     ar1[p] = ar0[...]
-    sum1 = [send(ar0, ar1.at[p], pdev(k)) for k in range(1, 8)]
-
-    first_stage(2)
-    for n in range(4):
-        stage1[0][n].wait_recv()
-    for m, sign in ((0, 1), (1, -1)):
-        block = ysend[0][lax.rem(z + 2 * sign + 8, 8)].astype(F32) + relay3[m].astype(F32)
-        acc[m, m] = (block[m] + relay4[m].astype(F32)).astype(BF)
-        acc[m, 1 - m] = block[1 - m].astype(BF)
-        stage1[0].append(send(acc.at[m], yrecv[0].at[2 + m], zdev(2 * sign)))
+    first_stage(2, 0)
+    first_stage(2, 1)
+    relay(1)
 
     stage2 = []
 
     def second_stage(n):
         kind, start, width = GROUPS[n]
         half = width // 2
-        for copy in stage1[n][4:] if kind == "z" else stage1[n]:
-            copy.wait_recv()
+        for j in range(2):
+            arrived(stage1[n][j][4:] if kind == "z" else stage1[n][j])
         pieces = []
         for q in range(2):
             for o in range(2):
                 columns = slice(q * half, (q + 1) * half)
-                piece = jnp.sum(yrecv[n][:, o, :, columns].astype(F32), axis=0)
-                if kind == "z":
-                    piece = piece + ysend[n][z, o, :, columns].astype(F32)
-                pieces.append(piece.astype(BF))
+                for j in range(2):
+                    piece = jnp.sum(yrecv[n][j, :, o, :, columns].astype(F32), axis=0)
+                    if kind == "z":
+                        piece = piece + ysend[n][j, z, o, :, columns].astype(F32)
+                    pieces.append(piece.astype(BF))
         stacked = jnp.concatenate(pieces, axis=0)
         zsend[n][...] = nn(regroup, stacked).astype(BF).reshape(8, 16, half)
         me = p if kind == "z" else z
         copies = []
-        for k in range(1, 8):
+        for k in P_STEPS if kind == "z" else Z_STEPS:
             to = pidx(k) if kind == "z" else lax.rem(z + k, 8)
             copies.append(
                 send(zsend[n].at[to], zrecv[n].at[me], pdev(k) if kind == "z" else zdev(k))
@@ -311,7 +331,16 @@
         copy.wait_recv()
     ar1s[...] = jnp.sum(ar1[...].astype(F32), axis=0).astype(BF)
     ar2[z] = ar1s[...]
-    sum2 = [send(ar1s, ar2.at[z], zdev(k)) for k in range(1, 8)]
+    sum2 = [send(ar1s, ar2.at[z], zdev(k)) for k in Z_STEPS]
+    for j in range(2):
+        gup[own[j], :] = e2[j]
+    pair_c.wait_recv()
+    for j in range(2):
+        gup[other[j], :] = er2[j]
+    wide_copy = pltpu.make_async_copy(lw_v, wide_out, osem.at[1])
+    wide_copy.start()
+    gup_copy = pltpu.make_async_copy(gup, gup_out, osem.at[2])
+    gup_copy.start()
     second_stage(0)
     second_stage(1)
     for copy in sum2:
@@ -378,7 +407,7 @@
         copy.wait()
 
 
-COPIES = 2 * (14 + 11 + 4) + 6 + 17 + 14 * len(GROUPS) + 1
+COPIES = 2 * (14 + 11 + 4) + 6 + 3 + 16 + 28 + 21 + 17
 
 
 def body(tokens, token_adapter_index, gate, up, down, imaps, omaps, cotangent):
@@ -391,20 +420,20 @@
         v((2048, 256), BF), v((2048, 256), BF), v((256, 2048), BF), v((256, 2048), BF), v((256, 256), BF),
         v((8, 8, 16, 256), BF), v((8, 8, 16, 256), BF), v((8, 8, 16, 256), BF), v((8, 8, 16, 256), BF),
         v((256, 2048), BF), v((256, 2048), BF),
-        v((256, 640), F32), v((128, 640), BF), v((128, 640), BF), v((128, 640), BF), v((128, 640), BF),
-        v((128, 640), BF), v((128, 640), BF),
-        v((256, 256), F32), v((128, 256), BF), v((128, 256), BF), v((128, 256), BF), v((128, 256), BF),
-        v((128, 256), BF), v((128, 256), BF),
-        v((128, 256), F32), v((256, 256), BF), v((256, 256), BF), v((256, 256), BF), v((256, 256), BF),
+        v((256, 640), F32), v((2, 64, 640), BF), v((2, 64, 640), BF), v((2, 64, 640), BF), v((2, 64, 640), BF),
+        v((2, 64, 640), BF), v((2, 64, 640), BF),
+        v((256, 256), F32), v((2, 64, 256), BF), v((2, 64, 256), BF), v((2, 64, 256), BF), v((2, 64, 256), BF),
+        v((2, 64, 256), BF), v((2, 64, 256), BF),
+        v((2, 64, 256), F32), v((256, 256), BF), v((256, 256), BF), v((256, 256), BF), v((256, 256), BF),
         v((256, 256), BF), v((256, 256), BF), v((256, 256), BF),
         v((32, 128), BF), v((8, 32, 128), BF), v((32, 128), BF), v((8, 32, 128), BF), v((32, 128), BF),
         v((4, 32, 128), BF),
     ]
-    scratch += [v((8, 2, 32, w), BF) for _, _, w in GROUPS]
-    scratch += [v((4 if kind == "z" else 8, 2, 32, w), BF) for kind, _, w in GROUPS]
+    scratch += [v((2, 8, 2, 16, w), BF) for _, _, w in GROUPS]
+    scratch += [v((2, 4 if kind == "z" else 8, 2, 16, w), BF) for kind, _, w in GROUPS]
     scratch += [v((8, 16, w // 2), BF) for _, _, w in GROUPS] * 2
     first = GROUPS[0][2]
-    scratch += [v((2, 2, 32, first), BF), v((2, 32, first), BF), v((2, 2, 32, first), BF)]
+    scratch += [v((2, 2, 2, 16, first), BF), v((2, 2, 16, first), BF), v((2, 2, 2, 16, first), BF)]
     scratch += [
         pltpu.SemaphoreType.DMA((5,)),
         pltpu.SemaphoreType.DMA((COPIES,)),

time: 69 us -> 66.3 us (0.961)
  Pallas kernels: 67.5 us -> 65.4 us
    pallas_call x1, Pallas kernels: 64.2 us -> 62.1 us  [body(): pl.pallas_call(kernel, out_shape=(jax.ShapeDtypeStruct((4, width), BF), j...]
where the time goes in v3:
time: 66.3 us; the launch traced here: 66.1 us
  Pallas kernels  65.4 us (99%)
    pallas_call x1, Pallas kernels, body(): pl.pallas_call(kernel, out_shape=(jax.ShapeDtypeStruct((4, width), BF), j...  62.1 us
    pallas_call x1, Pallas kernels, body(): pl.pallas_call(gradients, out_shape=(jax.ShapeDtypeStruct((4, width), BF)...  3.3 us

profile of v3, /device:TPU:32, one launch (start us, length us, event | category | flops | bytes accessed | tf_op | source)
XLA Modules:
  0.0 66.1 jit_solution(4008412826510126402)
XLA Ops:
  0.6 62.1 %layer.1 = (bf16[4,2048]{1,0:T(4,128)(2,1)}, bf16[4,2048]{1,0:T(4,128)(2,1)}, bf16[256,256]{1,0:T(8,128)(2,1)}, bf16[256,2048]{1,0:T(8,128)(2,1)}, bf16[256,256]{1,0:T(8,128)(2,1)}, /*index=5*/bf16[256,256]{1,0:T(8,128)(2,1)}) custom-call(s32[1,256]{1,0:T(1,128)} %bitcast.7, bf16[4,2048]{1,0:T(4,128)(2,1)} %tok.1, bf16[4,2048]{1,0:T(4,128)(2,1)} %cot.1, ...), custom_call_target="tpu_custom_call" | custom-call | tf_op jit(solution)/shard_map/layer/pallas_call | solution.py:443
  62.8 3.3 %gradients.1 = (bf16[4,2048]{1,0:T(4,128)(2,1)}, bf16[4,2048]{1,0:T(4,128)(2,1)}, f32[256,2048]{1,0:T(8,128)}, f32[256,256]{1,0:T(8,128)}) custom-call(bf16[4,2048]{1,0:T(4,128)(2,1)} %get-tuple-element.14.ref_in, bf16[4,2048]{1,0:T(4,128)(2,1)} %get-tuple-element.15.pol_in, bf16[256,256]{1,0:T(8,128)(2,1)} %get-tuple-element.16.back, ...), custom_call_target="tpu_custom_call" | custom-call | tf_op jit(solution)/shard_map/gradients/pallas_call | solution.py:470

commit v4 on v3

--- a/solution.py
+++ b/solution.py
@@ -332,6 +332,8 @@
     ar1s[...] = jnp.sum(ar1[...].astype(F32), axis=0).astype(BF)
     ar2[z] = ar1s[...]
     sum2 = [send(ar1s, ar2.at[z], zdev(k)) for k in Z_STEPS]
+    second_stage(0)
+    second_stage(1)
     for j in range(2):
         gup[own[j], :] = e2[j]
     pair_c.wait_recv()
@@ -341,14 +343,12 @@
     wide_copy.start()
     gup_copy = pltpu.make_async_copy(gup, gup_out, osem.at[2])
     gup_copy.start()
-    second_stage(0)
-    second_stage(1)
+    second_stage(2)
     for copy in sum2:
         copy.wait_recv()
     ar2s[...] = jnp.sum(ar2[...].astype(F32), axis=0).astype(BF)
     ar3[t] = ar2s[...]
     sum3 = [send(ar2s, ar3.at[t], tdev(k)) for k in range(1, 4)]
-    second_stage(2)
     for copy in sum3:
         copy.wait_recv()
     wides = []
@@ -380,11 +380,11 @@
 ):
     sources = [back, wide, gup, ref_in, pol_in] + [xt.at[:, pl.ds(k * 512, 512)] for k in range(4)]
     places = [bv, wv, uv, rv, pv] + [xv.at[k] for k in range(4)]
-    loads = []
-    for n in range(9):
+    loads = {}
+    for n in (0, 5, 6, 7, 8, 3, 4, 1, 2):
         load = pltpu.make_async_copy(sources[n], places[n], isem.at[n])
         load.start()
-        loads.append(load)
+        loads[n] = load
     stores = []
 
     def store(src, dst):

time: 66.3 us -> 65.5 us (0.988)
  Pallas kernels: 65.4 us -> 64.4 us
    pallas_call x1, Pallas kernels: 62.1 us -> 61.3 us  [body(): pl.pallas_call(kernel, out_shape=(jax.ShapeDtypeStruct((4, width), BF), j...]
where the time goes in v4:
time: 65.5 us; the launch traced here: 65.1 us
  Pallas kernels  64.4 us (98%)
    pallas_call x1, Pallas kernels, body(): pl.pallas_call(kernel, out_shape=(jax.ShapeDtypeStruct((4, width), BF), j...  61.3 us
    pallas_call x1, Pallas kernels, body(): pl.pallas_call(gradients, out_shape=(jax.ShapeDtypeStruct((4, width), BF)...  3.15 us

profile of v4, /device:TPU:32, one launch (start us, length us, event | category | flops | bytes accessed | tf_op | source)
XLA Modules:
  0.0 65.1 jit_solution(3337994784379542572)
XLA Ops:
  0.6 61.3 %layer.1 = (bf16[4,2048]{1,0:T(4,128)(2,1)}, bf16[4,2048]{1,0:T(4,128)(2,1)}, bf16[256,256]{1,0:T(8,128)(2,1)}, bf16[256,2048]{1,0:T(8,128)(2,1)}, bf16[256,256]{1,0:T(8,128)(2,1)}, /*index=5*/bf16[256,256]{1,0:T(8,128)(2,1)}) custom-call(s32[1,256]{1,0:T(1,128)} %bitcast.7, bf16[4,2048]{1,0:T(4,128)(2,1)} %tok.1, bf16[4,2048]{1,0:T(4,128)(2,1)} %cot.1, ...), custom_call_target="tpu_custom_call" | custom-call | tf_op jit(solution)/shard_map/layer/pallas_call | solution.py:443
  61.9 3.1 %gradients.1 = (bf16[4,2048]{1,0:T(4,128)(2,1)}, bf16[4,2048]{1,0:T(4,128)(2,1)}, f32[256,2048]{1,0:T(8,128)}, f32[256,256]{1,0:T(8,128)}) custom-call(bf16[4,2048]{1,0:T(4,128)(2,1)} %get-tuple-element.14.ref_in, bf16[4,2048]{1,0:T(4,128)(2,1)} %get-tuple-element.15.pol_in, bf16[256,256]{1,0:T(8,128)(2,1)} %get-tuple-element.16.back, ...), custom_call_target="tpu_custom_call" | custom-call | tf_op jit(solution)/shard_map/gradients/pallas_call | solution.py:470

commit v5 on v4

--- a/solution.py
+++ b/solution.py
@@ -201,8 +201,6 @@
     for j in range(2):
         s1[j] = f1[other[j], :].astype(BF)
         core_t.append(send(s1.at[j], r1.at[j], tdev(1)))
-    xt_copy = pltpu.make_async_copy(xt, xt_out, osem.at[0])
-    xt_copy.start()
     line_0 = to_line(0, core_t[0])
     line_1 = to_line(1, core_t[1])
     far_c = far_hops(ca, near_c)
@@ -267,11 +265,14 @@
             acc[j, m, 1 - m] = block[1 - m].astype(BF)
             stage1[0][j].append(send(acc.at[j, m], yrecv[0].at[j, 2 + m], zdev(2 * sign)))
 
+    xt_copy = pltpu.make_async_copy(xt, xt_out, osem.at[0])
+    xt_copy.start()
     pair_0 = activate(0, line_0)
+    arrived(plane_c)
+    unpack(cb, 1, ct)
     pair_1 = activate(1, line_1)
-    arrived(near_c[2:] + plane_c + far_c)
+    arrived(near_c[2:] + far_c)
     unpack(ca, 0, ct)
-    unpack(cb, 1, ct)
     f2[...] = nt(ct[...], down_v[...])
     for j in range(2):
         g1[j] = f2[other[j], :].astype(BF)

time: 65.5 us -> 65.3 us (level)
  no operation moved by 1% of the time
where the time goes in v5:
time: 65.3 us; the launch traced here: 64.8 us
  Pallas kernels  64.2 us (98%)
    pallas_call x1, Pallas kernels, body(): pl.pallas_call(kernel, out_shape=(jax.ShapeDtypeStruct((4, width), BF), j...  61 us
    pallas_call x1, Pallas kernels, body(): pl.pallas_call(gradients, out_shape=(jax.ShapeDtypeStruct((4, width), BF)...  3.14 us

profile of v5, /device:TPU:32, one launch (start us, length us, event | category | flops | bytes accessed | tf_op | source)
XLA Modules:
  0.0 64.8 jit_solution(8978644699013477487)
XLA Ops:
  0.6 61.0 %layer.1 = (bf16[4,2048]{1,0:T(4,128)(2,1)}, bf16[4,2048]{1,0:T(4,128)(2,1)}, bf16[256,256]{1,0:T(8,128)(2,1)}, bf16[256,2048]{1,0:T(8,128)(2,1)}, bf16[256,256]{1,0:T(8,128)(2,1)}, /*index=5*/bf16[256,256]{1,0:T(8,128)(2,1)}) custom-call(s32[1,256]{1,0:T(1,128)} %bitcast.7, bf16[4,2048]{1,0:T(4,128)(2,1)} %tok.1, bf16[4,2048]{1,0:T(4,128)(2,1)} %cot.1, ...), custom_call_target="tpu_custom_call" | custom-call | tf_op jit(solution)/shard_map/layer/pallas_call | solution.py:444
  61.7 3.1 %gradients.1 = (bf16[4,2048]{1,0:T(4,128)(2,1)}, bf16[4,2048]{1,0:T(4,128)(2,1)}, f32[256,2048]{1,0:T(8,128)}, f32[256,256]{1,0:T(8,128)}) custom-call(bf16[4,2048]{1,0:T(4,128)(2,1)} %get-tuple-element.14.ref_in, bf16[4,2048]{1,0:T(4,128)(2,1)} %get-tuple-element.15.pol_in, bf16[256,256]{1,0:T(8,128)(2,1)} %get-tuple-element.16.back, ...), custom_call_target="tpu_custom_call" | custom-call | tf_op jit(solution)/shard_map/gradients/pallas_call | solution.py:471
